TPU v7x, 32 devices: a whole 2x2x4 slice. The times are simulated.
32 devices in a mesh: gx: 4 (over y, core), gy: 8 (over z, x).
Axes of the slice: x: 2, y: 2, z: 4, core: 2. Of those that a mesh axis runs over, the one named last changes fastest.
Arguments:
- start_vector: float32 [2, 16, 64, 1024], P(None, None, 'gx', 'gy'), may hold values from -6 to 6
- viscosity: float32 [16, 64, 1024], P(None, 'gx', 'gy'), may hold values from 0.1 to 10
- friction: float32 [16, 64, 1024], P(None, 'gx', 'gy'), may hold values from 0.5 to 5
- shifts: float32 [8], replicated, may hold values from 0.2 to 1.6, as said below
Outputs:
- orthonormal: float32 [9, 2, 16, 64, 1024], P(None, None, None, 'gx', 'gy')
- factor: float32 [9, 9], replicated
Inputs may be any that keep to these rules, and one draw needn't show every extreme that they name: The 8 shifts are distinct, one in each of 8 equal parts of the range.
All inputs are finite; a program needn't handle non-finite values.
Results may differ from a plain program's by a relative error of at most 0.00035.
Values sent between devices are 32-bit elements; how exact they have to be, the bound alone decides.
A program may use at most 128 MiB of HBM per device.

v0:
```python
import jax
import jax.numpy as jnp
from jax import lax
from jax.sharding import PartitionSpec as P

cross_gain = 1.0


def extended(shard, sides, width):
    for axis, dim in sides:
        peers, length = (lax.axis_size(axis), shard.shape[dim])
        up = [(i, (i + 1) % peers) for i in range(peers - 1)]
        down = [(j, i) for i, j in up]
        last = lax.slice_in_dim(shard, length - width, length, axis=dim)
        first = lax.slice_in_dim(shard, 0, width, axis=dim)
        before = lax.ppermute(last, axis, up)
        after = lax.ppermute(first, axis, down)
        shard = jnp.concatenate([before, shard, after], axis=dim)
    return shard


def neighbour_offsets():
    offsets = []
    for shift_z in (-1, 0, 1):
        for shift_x in (-1, 0, 1):
            for shift_y in (-1, 0, 1):
                distance = abs(shift_z) + abs(shift_x) + abs(shift_y)
                if distance == 0:
                    continue
                offsets.append((shift_z, shift_x, shift_y, 0.5 ** (distance - 1)))
    return offsets


def apply_operator(field_pad, eta_pad, friction, region_mask):
    levels = friction.shape[0]
    row_count = field_pad.shape[2] - 2
    col_count = field_pad.shape[3] - 2
    eta_z = jnp.pad(eta_pad, ((1, 1), (0, 0), (0, 0)))
    field_z = jnp.pad(field_pad, ((0, 0), (1, 1), (0, 0), (0, 0)))
    centre_eta = eta_pad[:, 1 : 1 + row_count, 1 : 1 + col_count]
    diagonal = friction
    summed = jnp.zeros((2, levels, row_count, col_count), jnp.float32)
    for shift_z, shift_x, shift_y, weight in neighbour_offsets():
        linkage = (
            weight
            * 0.5
            * (
                centre_eta
                + eta_z[
                    1 + shift_z : 1 + shift_z + levels,
                    1 + shift_x : 1 + shift_x + row_count,
                    1 + shift_y : 1 + shift_y + col_count,
                ]
            )
        )
        diagonal = diagonal + linkage
        summed = (
            summed
            + linkage[None]
            * field_z[
                :,
                1 + shift_z : 1 + shift_z + levels,
                1 + shift_x : 1 + shift_x + row_count,
                1 + shift_y : 1 + shift_y + col_count,
            ]
        )
    crossed = 0.25 * (
        field_pad[:, :, 2 : 2 + row_count, 2 : 2 + col_count]
        - field_pad[:, :, 2 : 2 + row_count, 0:col_count]
        - field_pad[:, :, 0:row_count, 2 : 2 + col_count]
        + field_pad[:, :, 0:row_count, 0:col_count]
    )
    centre = field_pad[:, :, 1 : 1 + row_count, 1 : 1 + col_count]
    safe_diag = jnp.where(region_mask > 0, diagonal, 1.0)
    result = centre - (summed - cross_gain * centre_eta[None] * crossed[::-1]) / safe_diag
    return result * region_mask


def lower_inverse(factor_low):
    order_n = factor_low.shape[0]
    identity = jnp.eye(order_n, dtype=jnp.float32)
    inverse = jnp.zeros((order_n, order_n), jnp.float32)
    for position in range(order_n):
        earlier = jnp.dot(
            factor_low[position, :position], inverse[:position], precision=lax.Precision.HIGHEST
        )
        inverse = inverse.at[position].set(
            (identity[position] - earlier) / factor_low[position, position]
        )
    return inverse


def cholesky_pass(basis_rows, gram):
    factor_low = jnp.linalg.cholesky(gram)
    return (
        jnp.dot(lower_inverse(factor_low), basis_rows, precision=lax.Precision.HIGHEST),
        factor_low,
    )


def on_device(start_vector, viscosity, friction, shifts):
    levels, row_count, col_count = viscosity.shape
    powers = shifts.shape[0]
    total_count = 2 * levels * row_count * lax.axis_size("gx") * col_count * lax.axis_size("gy")
    krylov = [start_vector]
    coeffs = jnp.stack([viscosity, friction])
    widened = extended(coeffs, (("gx", 2), ("gy", 3)), powers + 1)
    current = extended(start_vector, (("gx", 2), ("gy", 3)), powers)
    row_pos = (
        lax.axis_index("gx") * row_count - (powers + 1) + jnp.arange(row_count + 2 * powers + 2)
    )
    col_pos = (
        lax.axis_index("gy") * col_count - (powers + 1) + jnp.arange(col_count + 2 * powers + 2)
    )
    row_in = (row_pos >= 0) & (row_pos < row_count * lax.axis_size("gx"))
    col_in = (col_pos >= 0) & (col_pos < col_count * lax.axis_size("gy"))
    inside = (row_in[:, None] & col_in[None, :]).astype(jnp.float32)
    for power in range(powers):
        margin = powers - power
        eta_pad = widened[0][
            :,
            power + 1 : power + 1 + row_count + 2 * margin,
            power + 1 : power + 1 + col_count + 2 * margin,
        ]
        fric_part = widened[1][
            :,
            power + 2 : power + row_count + 2 * margin,
            power + 2 : power + col_count + 2 * margin,
        ]
        region = inside[
            power + 2 : power + row_count + 2 * margin, power + 2 : power + col_count + 2 * margin
        ]
        applied = apply_operator(current, eta_pad, fric_part, region)
        current = applied - shifts[power] * current[:, :, 1:-1, 1:-1]
        krylov.append(
            current[:, :, margin - 1 : margin - 1 + row_count, margin - 1 : margin - 1 + col_count]
        )

    def global_gram(basis_rows):
        partial_value = jnp.dot(basis_rows, basis_rows.T, precision=lax.Precision.HIGHEST)
        summed = lax.psum(partial_value, ("gx", "gy"))
        return summed / total_count

    basis_rows = jnp.stack(krylov).reshape(powers + 1, -1)
    ortho_one, low_one = cholesky_pass(basis_rows, global_gram(basis_rows))
    ortho_two, low_two = cholesky_pass(ortho_one, global_gram(ortho_one))
    factor = jnp.dot(low_two.T, low_one.T, precision=lax.Precision.HIGHEST)
    return (ortho_two.reshape(powers + 1, 2, levels, row_count, col_count), factor)


def solution(mesh):
    return jax.shard_map(
        on_device,
        mesh=mesh,
        in_specs=(P(None, None, "gx", "gy"), P(None, "gx", "gy"), P(None, "gx", "gy"), P()),
        out_specs=(P(None, None, None, "gx", "gy"), P()),
        check_vma=False,
    )
```

profile of v0, /device:TPU:0, one launch (start us, length us, event | category | flops | bytes accessed | tf_op | source)
XLA Modules:
  0.0 433.7 jit_solution(16997418263096803367)
XLA Ops:
  8.0 5.8 %collective-permute-start.4 = (f32[2,16,9,128]{3,1,2,0:T(8,128)S(1)}, f32[2,16,9,128]{3,1,2,0:T(8,128)S(1)}, u32[]{:S(2)}, u32[]{:S(2)}) collective-permute-start(f32[2,16,9,128]{3,1,2,0:T(8,128)S(1)} %copy.750), channel_id=1, source_target_pairs={{0,8},{8,16},{16,24},{1,9},{9,17},{17,25},{2,10},{10,18},{18,26},{... | collective-permute-start | bytes 442376 | tf_op jit(solution)/shard_map/ppermute | solution.py:16
  29.2 5.3 %collective-permute-start.2 = (f32[2,16,32,8]{3,2,1,0:T(8,128)}, f32[2,16,32,8]{3,2,1,0:T(8,128)}, u32[]{:S(2)}, u32[]{:S(2)}) collective-permute-start(f32[2,16,32,8]{3,2,1,0:T(8,128)} %get-tuple-element.459), channel_id=1, source_target_pairs={{0,1},{1,2},{2,3},{3,4},{4,5},{5,6},{6,7},{8,9},{9,10},{10,11},{11... | collective-permute-start | bytes 98312 | tf_op jit(solution)/shard_map/ppermute | solution.py:16
  38.8 4.0 pad_maximum_fusion
  46.6 5.2 %collective-permute-start.6 = (f32[2,16,34,9]{2,1,3,0:T(8,128)}, f32[2,16,34,9]{2,1,3,0:T(8,128)}, u32[]{:S(2)}, u32[]{:S(2)}) collective-permute-start(f32[2,16,34,9]{2,1,3,0:T(8,128)} %get-tuple-element.439), channel_id=1, source_target_pairs={{0,1},{1,2},{2,3},{3,4},{4,5},{5,6},{6,7},{8,9},{9,10},{10,11},{11... | collective-permute-start | bytes 117512 | tf_op jit(solution)/shard_map/ppermute | solution.py:16
  51.8 7.3 %collective-permute-done.2 = f32[2,16,32,8]{3,2,1,0:T(8,128)} collective-permute-done((f32[2,16,32,8]{3,2,1,0:T(8,128)}, f32[2,16,32,8]{3,2,1,0:T(8,128)}, u32[]{:S(2)}, u32[]{:S(2)}) %collective-permute-start.2) | collective-permute-done | bytes 32800 | tf_op jit(solution)/shard_map/ppermute | solution.py:16
  65.7 3.9 add_select_fusion
  100.4 9.3 %multiply_subtract_fusion.2 = f32[2,16,30,142]{3,2,1,0:T(8,128)S(1)} fusion(f32[2,16,32,144]{3,2,1,0:T(8,128)S(1)} %pad_maximum_fusion.2, f32[2,16,30,142]{3,2,1,0:T(8,128)} %subtract_add_fusion.2, f32[]{:T(128)} %bitcast.5, f32[30,142]{1,0:T(8,128)} %slice.2712, f32[16,30,142]{2,1,0:T(8,128)} %copy.539, f32[16,30,142]{2,1,0:T(8,128)} %copy.538, ...), kind=kLoop, calls=%fused_computation.430 | loop fusion | flops 7906560 | bytes 19227284 | tf_op jit(solution)/shard_map/sub | solution.py:134
  113.1 3.3 add_select_fusion.1
  146.5 9.2 %multiply_subtract_fusion.1 = f32[2,16,28,140]{3,2,1,0:T(8,128)S(1)} fusion(f32[2,16,30,142]{3,2,1,0:T(8,128)S(1)} %multiply_subtract_fusion.2, f32[2,16,28,140]{3,2,1,0:T(8,128)} %subtract_add_fusion.1, f32[]{:T(128)} %bitcast.8, f32[28,140]{1,0:T(8,128)S(1)} %slice.2734, f32[16,28,140]{2,1,0:T(8,128)} %copy.567, f32[16,28,140]{2,1,0:T(8,128)} %copy.566, ...), kind=kLoop, calls=%fused_computation.428 | loop fusion | flops 7275520 | bytes 18546692 | tf_op jit(solution)/shard_map/sub | solution.py:134
  159.0 3.0 add_select_fusion.2
  191.5 9.4 %multiply_subtract_fusion = f32[2,16,26,138]{3,2,1,0:T(8,128)S(1)} fusion(f32[2,16,28,140]{3,2,1,0:T(8,128)S(1)} %multiply_subtract_fusion.1, f32[2,16,26,138]{3,2,1,0:T(8,128)} %subtract_add_fusion, f32[]{:T(128)} %bitcast.11, f32[26,138]{1,0:T(8,128)S(1)} %slice.2755, f32[16,26,138]{2,1,0:T(8,128)} %copy.595, f32[16,26,138]{2,1,0:T(8,128)} %copy.594, ...), kind=kLoop, calls=%fused_computation.426 | loop fusion | flops 6659328 | bytes 17866756 | tf_op jit(solution)/shard_map/sub | solution.py:134
  202.1 2.7 add_select_fusion.3
  222.1 6.2 %multiply_subtract_fusion.6 = f32[2,16,24,136]{3,2,1,0:T(8,128)S(1)} fusion(f32[2,16,26,138]{3,2,1,0:T(8,128)S(1)} %multiply_subtract_fusion, f32[2,16,24,136]{3,2,1,0:T(8,128)S(1)} %subtract_add_fusion.6, f32[]{:T(128)} %bitcast.14, f32[24,136]{1,0:T(8,128)S(1)} %copy-done.17, f32[16,24,136]{2,1,0:T(8,128)S(1)} %copy.623, f32[16,24,136]{2,1,0:T(8,128)S(1)} %copy.622, ...), kind=kLoop, calls=%fused_computation.710 | loop fusion | flops 6057984 | bytes 18890756 | tf_op jit(solution)/shard_map/sub | solution.py:134
  237.9 4.8 %multiply_subtract_fusion.5 = f32[2,16,22,134]{3,2,1,0:T(8,128)S(1)} fusion(f32[2,16,24,136]{3,2,1,0:T(8,128)S(1)} %multiply_subtract_fusion.6, f32[2,16,22,134]{3,2,1,0:T(8,128)S(1)} %subtract_add_fusion.5, f32[]{:T(128)} %bitcast.17, f32[22,134]{1,0:T(8,128)S(1)} %copy-done.16, f32[16,22,134]{2,1,0:T(8,128)S(1)} %copy.651, f32[16,22,134]{2,1,0:T(8,128)S(1)} %copy.650, ...), kind=kLoop, calls=%fused_computation.708 | loop fusion | flops 5471488 | bytes 20062724 | tf_op jit(solution)/shard_map/sub | solution.py:134
  251.6 5.1 %multiply_subtract_fusion.4 = f32[2,16,20,132]{3,2,1,0:T(8,128)S(1)} fusion(f32[2,16,22,134]{3,2,1,0:T(8,128)S(1)} %multiply_subtract_fusion.5, f32[2,16,20,132]{3,2,1,0:T(8,128)S(1)} %subtract_add_fusion.4, f32[]{:T(128)} %bitcast.20, f32[20,132]{1,0:T(8,128)S(1)} %copy-done.15, f32[16,20,132]{2,1,0:T(8,128)S(1)} %copy.679, f32[16,20,132]{2,1,0:T(8,128)S(1)} %copy.678, ...), kind=kLoop, calls=%fused_computation.706 | loop fusion | flops 4899840 | bytes 20023300 | tf_op jit(solution)/shard_map/sub | solution.py:134
  264.6 4.8 %multiply_subtract_fusion.3 = f32[2,16,18,130]{3,2,1,0:T(8,128)S(1)} fusion(f32[2,16,20,132]{3,2,1,0:T(8,128)S(1)} %multiply_subtract_fusion.4, f32[2,16,18,130]{3,2,1,0:T(8,128)S(1)} %subtract_add_fusion.3, f32[]{:T(128)} %bitcast.23, f32[18,130]{1,0:T(8,128)S(1)} %copy-done.14, f32[16,18,130]{2,1,0:T(8,128)S(1)} %copy.707, f32[16,18,130]{2,1,0:T(8,128)S(1)} %copy.706, ...), kind=kLoop, calls=%fused_computation.704 | loop fusion | flops 4343040 | bytes 19984900 | tf_op jit(solution)/shard_map/sub | solution.py:134
  274.0 8.0 %stack.71 = f32[9,2,16,16,128]{4,0,3,2,1:T(8,128)} concatenate(f32[1,2,16,16,128]{4,0,3,2,1:T(1,128)S(1)} %bitcast.330, f32[1,2,16,16,128]{4,0,3,2,1:T(1,128)S(1)} %bitcast.336, f32[1,2,16,16,128]{4,0,3,2,1:T(1,128)S(1)} %bitcast.338, f32[1,2,16,16,128]{4,0,3,2,1:T(1,128)S(1)} %bitcast.340, f32[1,2,16,16,128]{4,0,3,2,1:T(1,128)S(1)} %bitcast.342, ...), dimensions={0} | concatenate | bytes 4718592 | tf_op jit(solution)/shard_map/stack | solution.py:144
  282.0 9.0 %convolution_bitcast_fusion = f32[9,9]{0,1:T(8,128)S(1)} fusion(f32[9,2,16,16,128]{4,0,3,2,1:T(8,128)} %stack.71), kind=kOutput, calls=%fused_computation.146 | convolution fusion | flops 63700992 | bytes 2359620 | tf_op jit(solution)/shard_map/dot_general | solution.py:140
  291.1 40.6 %psum.14 = f32[9,9]{0,1:T(8,128)S(1)} all-reduce(f32[9,9]{0,1:T(8,128)S(1)} %convolution_bitcast_fusion), channel_id=1, replica_groups=mesh['gx'=4,'gy'=8] {'gx','gy'}, use_global_device_ids=true, to_apply=%region_0.1 | all-reduce | flops 81 | bytes 648 | tf_op jit(solution)/shard_map/psum | solution.py:141
  347.5 8.1 %stack.81 = f32[9,65536]{1,0:T(8,128)} concatenate(f32[1,65536]{1,0:T(1,128)S(1)} %bitcast.331, f32[1,65536]{1,0:T(1,128)S(1)} %bitcast.337, f32[1,65536]{1,0:T(1,128)S(1)} %bitcast.339, f32[1,65536]{1,0:T(1,128)S(1)} %bitcast.341, f32[1,65536]{1,0:T(1,128)S(1)} %bitcast.343, f32[1,65536]{1,0:T(1,128)S(1)} %bitcast.345, f32[1,65536]{1,0:T(1,128)S(1)} %bitcast.347, ...), dimensions={0} | concatenate | bytes 4718592 | tf_op jit(solution)/shard_map/stack | solution.py:144
  355.6 5.4 %fusion.1195 = f32[9,65536]{1,0:T(8,128)S(1)} fusion(f32[9,9]{1,0:T(8,128)S(1)} %scatter.74, f32[9,65536]{1,0:T(8,128)} %stack.81), kind=kOutput, calls=%fused_computation.1486 | convolution fusion | flops 63700992 | bytes 4718916 | tf_op jit(solution)/shard_map/dot_general | solution.py:96
  362.9 5.6 %fusion.1196 = f32[9,9]{0,1:T(8,128)S(1)} fusion(f32[9,65536]{1,0:T(8,128)S(1)} %fusion.1195), kind=kOutput, calls=%fused_computation.1487 | convolution fusion | flops 63700992 | bytes 2359620 | tf_op jit(solution)/shard_map/dot_general | solution.py:140
  368.5 40.6 %psum.15 = f32[9,9]{0,1:T(8,128)S(1)} all-reduce(f32[9,9]{0,1:T(8,128)S(1)} %fusion.1196), channel_id=1, replica_groups=mesh['gx'=4,'gy'=8] {'gx','gy'}, use_global_device_ids=true, to_apply=%region_3.5 | all-reduce | flops 81 | bytes 648 | tf_op jit(solution)/shard_map/psum | solution.py:141
  425.7 5.4 %fusion.1197 = f32[9,65536]{1,0:T(8,128)S(1)} fusion(f32[9,9]{1,0:T(8,128)S(1)} %scatter.89, f32[9,65536]{1,0:T(8,128)} %copy-done), kind=kOutput, calls=%fused_computation.1488 | convolution fusion | flops 63700992 | bytes 4718916 | tf_op jit(solution)/shard_map/dot_general | solution.py:96
  (415 shorter events, 219.1 us)
Async XLA Ops:
  1.6 25.0 %collective-permute-start = (f32[2,16,8,128]{3,2,1,0:T(8,128)S(1)}, f32[2,16,8,128]{3,2,1,0:T(8,128)S(1)}, u32[]{:S(2)}, u32[]{:S(2)}) collective-permute-start(f32[2,16,8,128]{3,2,1,0:T(8,128)S(1)} %get-tuple-element.464), channel_id=1, source_target_pairs={{0,8},{8,16},{16,24},{1,9},{9,17},{17,25},{2,10},{10,18},{18,26},{... | collective-permute-start | bytes 393224 | tf_op jit(solution)/shard_map/ppermute | solution.py:16
  4.0 22.7 %collective-permute-start.1 = (f32[2,16,8,128]{3,2,1,0:T(8,128)S(1)}, f32[2,16,8,128]{3,2,1,0:T(8,128)S(1)}, u32[]{:S(2)}, u32[]{:S(2)}) collective-permute-start(f32[2,16,8,128]{3,2,1,0:T(8,128)S(1)} %get-tuple-element.463), channel_id=1, source_target_pairs={{8,0},{16,8},{24,16},{9,1},{17,9},{25,17},{10,2},{18,10},{26,18},{... | collective-permute-start | bytes 393224 | tf_op jit(solution)/shard_map/ppermute | solution.py:17
  6.4 19.5 %copy-start.23 = (f32[8]{0:T(128)S(1)}, f32[8]{0:T(128)}, u32[]{:S(2)}) copy-start(f32[8]{0:T(128)} %param.44) | copy-start | bytes 100
  6.4 20.2 %copy-start.1 = (f32[2,16,16,128]{3,2,1,0:T(8,128)S(1)}, f32[2,16,16,128]{3,2,1,0:T(8,128)}, u32[]{:S(2)}) copy-start(f32[2,16,16,128]{3,2,1,0:T(8,128)} %param.41) | copy-start | bytes 786436
  6.5 28.0 %collective-permute-start.5 = (f32[2,16,9,128]{3,1,2,0:T(8,128)S(1)}, f32[2,16,9,128]{3,1,2,0:T(8,128)S(1)}, u32[]{:S(2)}, u32[]{:S(2)}) collective-permute-start(f32[2,16,9,128]{3,1,2,0:T(8,128)S(1)} %copy.751), channel_id=1, source_target_pairs={{8,0},{16,8},{24,16},{9,1},{17,9},{25,17},{10,2},{18,10},{26,18},{... | collective-permute-start | bytes 442376 | tf_op jit(solution)/shard_map/ppermute | solution.py:17
  8.0 28.6 %collective-permute-start.4 = (f32[2,16,9,128]{3,1,2,0:T(8,128)S(1)}, f32[2,16,9,128]{3,1,2,0:T(8,128)S(1)}, u32[]{:S(2)}, u32[]{:S(2)}) collective-permute-start(f32[2,16,9,128]{3,1,2,0:T(8,128)S(1)} %copy.750), channel_id=1, source_target_pairs={{0,8},{8,16},{16,24},{1,9},{9,17},{17,25},{2,10},{10,18},{18,26},{... | collective-permute-start | bytes 442376 | tf_op jit(solution)/shard_map/ppermute | solution.py:16
  27.9 24.0 %collective-permute-start.3 = (f32[2,16,32,8]{3,2,1,0:T(8,128)}, f32[2,16,32,8]{3,2,1,0:T(8,128)S(1)}, u32[]{:S(2)}, u32[]{:S(2)}) collective-permute-start(f32[2,16,32,8]{3,2,1,0:T(8,128)} %get-tuple-element.460), channel_id=1, source_target_pairs={{1,0},{2,1},{3,2},{4,3},{5,4},{6,5},{7,6},{9,8},{10,9},{11,10},{12... | collective-permute-start | bytes 98312 | tf_op jit(solution)/shard_map/ppermute | solution.py:17
  29.2 30.0 %collective-permute-start.2 = (f32[2,16,32,8]{3,2,1,0:T(8,128)}, f32[2,16,32,8]{3,2,1,0:T(8,128)}, u32[]{:S(2)}, u32[]{:S(2)}) collective-permute-start(f32[2,16,32,8]{3,2,1,0:T(8,128)} %get-tuple-element.459), channel_id=1, source_target_pairs={{0,1},{1,2},{2,3},{3,4},{4,5},{5,6},{6,7},{8,9},{9,10},{10,11},{11... | collective-permute-start | bytes 98312 | tf_op jit(solution)/shard_map/ppermute | solution.py:16
  45.3 16.9 %collective-permute-start.7 = (f32[2,16,34,9]{2,1,3,0:T(8,128)}, f32[2,16,34,9]{2,1,3,0:T(8,128)S(1)}, u32[]{:S(2)}, u32[]{:S(2)}) collective-permute-start(f32[2,16,34,9]{2,1,3,0:T(8,128)} %get-tuple-element.440), channel_id=1, source_target_pairs={{1,0},{2,1},{3,2},{4,3},{5,4},{6,5},{7,6},{9,8},{10,9},{11,10},{12... | collective-permute-start | bytes 117512 | tf_op jit(solution)/shard_map/ppermute | solution.py:17
  46.6 16.0 %collective-permute-start.6 = (f32[2,16,34,9]{2,1,3,0:T(8,128)}, f32[2,16,34,9]{2,1,3,0:T(8,128)}, u32[]{:S(2)}, u32[]{:S(2)}) collective-permute-start(f32[2,16,34,9]{2,1,3,0:T(8,128)} %get-tuple-element.439), channel_id=1, source_target_pairs={{0,1},{1,2},{2,3},{3,4},{4,5},{5,6},{6,7},{8,9},{9,10},{10,11},{11... | collective-permute-start | bytes 117512 | tf_op jit(solution)/shard_map/ppermute | solution.py:16
  60.6 3.3 copy-start.4
  110.5 2.6 copy-start.5
  156.5 2.5 copy-start.6
  217.6 4.4 %copy-start.8 = (f32[16,24,136]{2,1,0:T(8,128)S(1)}, f32[16,24,136]{2,1,0:T(8,128)}, u32[]{:S(2)}) copy-start(f32[16,24,136]{2,1,0:T(8,128)} %copy.611) | copy-start | bytes 626692
  217.6 4.4 %copy-start.9 = (f32[16,24,136]{2,1,0:T(8,128)S(1)}, f32[16,24,136]{2,1,0:T(8,128)}, u32[]{:S(2)}) copy-start(f32[16,24,136]{2,1,0:T(8,128)} %copy.610) | copy-start | bytes 626692
  217.6 4.4 %copy-start.10 = (f32[16,24,136]{2,1,0:T(8,128)S(1)}, f32[16,24,136]{2,1,0:T(8,128)}, u32[]{:S(2)}) copy-start(f32[16,24,136]{2,1,0:T(8,128)} %copy.609) | copy-start | bytes 626692
  217.6 4.4 %copy-start.17 = (f32[24,136]{1,0:T(8,128)S(1)}, f32[24,136]{1,0:T(8,128)}, u32[]{:S(2)}) copy-start(f32[24,136]{1,0:T(8,128)} %slice.2776) | copy-start | bytes 39172
  218.6 3.5 copy-start.11
  219.6 2.5 copy-start.12
  264.6 5.1 %copy-start.28 = (pred[16,128]{1,0:T(8,128)(4,1)S(1)}, pred[16,128]{1,0:T(8,128)(4,1)}, u32[]{:S(2)}) copy-start(pred[16,128]{1,0:T(8,128)(4,1)} %broadcast_compare_fusion.7) | copy-start | bytes 6148
  333.9 3.3 copy-start.18
  360.9 2.0 copy-start
  362.9 49.2 %copy-start.19 = (f32[9,9]{1,0:T(8,128)S(1)}, f32[9,9]{1,0:T(8,128)}, u32[]{:S(2)}) copy-start(f32[9,9]{1,0:T(8,128)} %copy-done.18) | copy-start | bytes 976
  411.4 4.2 copy-start.20
  (13 other events, 15.9 us)
where the time goes:
time: 442 us; the launch traced here: 434 us
  local copies, waits for them, and re-layouts  168 us (38%)
  other arithmetic  104 us (24%)
  blocking collectives  81.2 us (18%)
  matrix products  46.2 us (10%)
  starting transfers between devices  24 us (5%)
  waiting for transfers between devices  7.31 us (2%)
    mul x208, local copies, waits for them, and re-layouts, apply_operator(): weight * 0.5  117 us
    psum x2, blocking collectives, global_gram(): summed = lax.psum(partial_value, ('gx', 'gy'))  81.2 us
    sub x8, other arithmetic, on_device(): current = applied - shifts[power] * current[:, :, 1:-1, 1:-1]  50.7 us
    select_n x8, other arithmetic, apply_operator(): safe_diag = jnp.where(region_mask > 0, diagonal, 1.0)  20.3 us
    dot_general x14, matrix products, lower_inverse(): jnp.dot(factor_low[position, :position], inverse[:position], precision=la...  20 us
    ppermute x4, starting transfers between devices, extended(): before = lax.ppermute(last, axis, up)  18.7 us
    another operation x2, local copies, waits for them, and re-layouts, on_device(): basis_rows = jnp.stack(krylov).reshape(powers + 1, -1)  16.1 us
    dot_general x2, matrix products, global_gram(): jnp.dot(basis_rows, basis_rows.T, precision=lax.Precision.HIGHEST)  14.7 us
  transfers between devices with their start and end apart: 8, of which 1 were waited for; matrix products, arithmetic and copies ran while one was open for 7% of the time, Pallas kernels for 0%

commit v1 on v0

--- a/solution.py
+++ b/solution.py
@@ -138,7 +138,7 @@
 
     def global_gram(basis_rows):
         partial_value = jnp.dot(basis_rows, basis_rows.T, precision=lax.Precision.HIGHEST)
-        summed = lax.psum(partial_value, ("gx", "gy"))
+        summed = lax.psum(lax.psum(partial_value, "gy"), "gx")
         return summed / total_count
 
     basis_rows = jnp.stack(krylov).reshape(powers + 1, -1)

time: 442 us -> 412 us (0.932)
  blocking collectives: 81.2 us -> 49.2 us
    psum x2 -> x4, blocking collectives: 81.2 us -> 49.2 us  [global_gram(): summed = lax.psum(lax.psum(partial_value, 'gy'), 'gx')]
where the time goes in v1:
time: 412 us; the launch traced here: 404 us
  local copies, waits for them, and re-layouts  168 us (41%)
  other arithmetic  106 us (26%)
  blocking collectives  49.2 us (12%)
  matrix products  46.5 us (11%)
  starting transfers between devices  23.4 us (6%)
  waiting for transfers between devices  8.77 us (2%)
    mul x208, local copies, waits for them, and re-layouts, apply_operator(): weight * 0.5  118 us
    sub x8, other arithmetic, on_device(): current = applied - shifts[power] * current[:, :, 1:-1, 1:-1]  50.9 us
    psum x4, blocking collectives, global_gram(): summed = lax.psum(lax.psum(partial_value, 'gy'), 'gx')  49.2 us
    dot_general x14, matrix products, lower_inverse(): jnp.dot(factor_low[position, :position], inverse[:position], precision=la...  20.3 us
    select_n x8, other arithmetic, apply_operator(): safe_diag = jnp.where(region_mask > 0, diagonal, 1.0)  20.2 us
    ppermute x4, starting transfers between devices, extended(): before = lax.ppermute(last, axis, up)  18.1 us
    another operation x2, local copies, waits for them, and re-layouts, on_device(): basis_rows = jnp.stack(krylov).reshape(powers + 1, -1)  16 us
    dot_general x2, matrix products, global_gram(): jnp.dot(basis_rows, basis_rows.T, precision=lax.Precision.HIGHEST)  14.6 us
  transfers between devices with their start and end apart: 8, of which 1 were waited for; matrix products, arithmetic and copies ran while one was open for 7% of the time, Pallas kernels for 0%

profile of v1, /device:TPU:0, one launch (start us, length us, event | category | flops | bytes accessed | tf_op | source)
XLA Modules:
  0.0 404.1 jit_solution(13354014796773766593)
XLA Ops:
  8.0 5.8 %collective-permute-start.4 = (f32[2,16,9,128]{3,1,2,0:T(8,128)S(1)}, f32[2,16,9,128]{3,1,2,0:T(8,128)S(1)}, u32[]{:S(2)}, u32[]{:S(2)}) collective-permute-start(f32[2,16,9,128]{3,1,2,0:T(8,128)S(1)} %copy.750), channel_id=1, source_target_pairs={{0,8},{8,16},{16,24},{1,9},{9,17},{17,25},{2,10},{10,18},{18,26},{... | collective-permute-start | bytes 442376 | tf_op jit(solution)/shard_map/ppermute | solution.py:16
  29.1 5.4 %collective-permute-start.2 = (f32[2,16,32,8]{3,2,1,0:T(8,128)}, f32[2,16,32,8]{3,2,1,0:T(8,128)}, u32[]{:S(2)}, u32[]{:S(2)}) collective-permute-start(f32[2,16,32,8]{3,2,1,0:T(8,128)} %get-tuple-element.459), channel_id=1, source_target_pairs={{0,1},{1,2},{2,3},{3,4},{4,5},{5,6},{6,7},{8,9},{9,10},{10,11},{11... | collective-permute-start | bytes 98312 | tf_op jit(solution)/shard_map/ppermute | solution.py:16
  38.8 4.0 pad_maximum_fusion
  45.8 4.6 %collective-permute-start.6 = (f32[2,16,34,9]{2,1,3,0:T(8,128)}, f32[2,16,34,9]{2,1,3,0:T(8,128)S(1)}, u32[]{:S(2)}, u32[]{:S(2)}) collective-permute-start(f32[2,16,34,9]{2,1,3,0:T(8,128)} %get-tuple-element.439), channel_id=1, source_target_pairs={{0,1},{1,2},{2,3},{3,4},{4,5},{5,6},{6,7},{8,9},{9,10},{10,11},{11... | collective-permute-start | bytes 117512 | tf_op jit(solution)/shard_map/ppermute | solution.py:16
  50.4 8.8 %collective-permute-done.2 = f32[2,16,32,8]{3,2,1,0:T(8,128)} collective-permute-done((f32[2,16,32,8]{3,2,1,0:T(8,128)}, f32[2,16,32,8]{3,2,1,0:T(8,128)}, u32[]{:S(2)}, u32[]{:S(2)}) %collective-permute-start.2) | collective-permute-done | bytes 32800 | tf_op jit(solution)/shard_map/ppermute | solution.py:16
  66.8 3.9 add_select_fusion
  101.4 9.3 %multiply_subtract_fusion.2 = f32[2,16,30,142]{3,2,1,0:T(8,128)S(1)} fusion(f32[2,16,32,144]{3,2,1,0:T(8,128)S(1)} %pad_maximum_fusion.2, f32[2,16,30,142]{3,2,1,0:T(8,128)} %subtract_add_fusion.2, f32[]{:T(128)} %bitcast.5, f32[30,142]{1,0:T(8,128)} %slice.2712, f32[16,30,142]{2,1,0:T(8,128)} %copy.539, f32[16,30,142]{2,1,0:T(8,128)} %copy.538, ...), kind=kLoop, calls=%fused_computation.430 | loop fusion | flops 7906560 | bytes 19227284 | tf_op jit(solution)/shard_map/sub | solution.py:134
  114.1 3.3 add_select_fusion.1
  147.3 9.3 %multiply_subtract_fusion.1 = f32[2,16,28,140]{3,2,1,0:T(8,128)S(1)} fusion(f32[2,16,30,142]{3,2,1,0:T(8,128)S(1)} %multiply_subtract_fusion.2, f32[2,16,28,140]{3,2,1,0:T(8,128)} %subtract_add_fusion.1, f32[]{:T(128)} %bitcast.8, f32[28,140]{1,0:T(8,128)S(1)} %slice.2734, f32[16,28,140]{2,1,0:T(8,128)} %copy.567, f32[16,28,140]{2,1,0:T(8,128)} %copy.566, ...), kind=kLoop, calls=%fused_computation.428 | loop fusion | flops 7275520 | bytes 18546692 | tf_op jit(solution)/shard_map/sub | solution.py:134
  192.5 9.5 %multiply_subtract_fusion = f32[2,16,26,138]{3,2,1,0:T(8,128)S(1)} fusion(f32[2,16,28,140]{3,2,1,0:T(8,128)S(1)} %multiply_subtract_fusion.1, f32[2,16,26,138]{3,2,1,0:T(8,128)} %subtract_add_fusion, f32[]{:T(128)} %bitcast.11, f32[26,138]{1,0:T(8,128)S(1)} %slice.2755, f32[16,26,138]{2,1,0:T(8,128)} %copy.595, f32[16,26,138]{2,1,0:T(8,128)} %copy.594, ...), kind=kLoop, calls=%fused_computation.426 | loop fusion | flops 6659328 | bytes 17866756 | tf_op jit(solution)/shard_map/sub | solution.py:134
  223.9 6.2 %multiply_subtract_fusion.6 = f32[2,16,24,136]{3,2,1,0:T(8,128)S(1)} fusion(f32[2,16,26,138]{3,2,1,0:T(8,128)S(1)} %multiply_subtract_fusion, f32[2,16,24,136]{3,2,1,0:T(8,128)S(1)} %subtract_add_fusion.6, f32[]{:T(128)} %bitcast.14, f32[24,136]{1,0:T(8,128)S(1)} %copy-done.17, f32[16,24,136]{2,1,0:T(8,128)S(1)} %copy.623, f32[16,24,136]{2,1,0:T(8,128)S(1)} %copy.622, ...), kind=kLoop, calls=%fused_computation.710 | loop fusion | flops 6057984 | bytes 18706436 | tf_op jit(solution)/shard_map/sub | solution.py:134
  239.7 4.9 %multiply_subtract_fusion.5 = f32[2,16,22,134]{3,2,1,0:T(8,128)S(1)} fusion(f32[2,16,24,136]{3,2,1,0:T(8,128)S(1)} %multiply_subtract_fusion.6, f32[2,16,22,134]{3,2,1,0:T(8,128)S(1)} %subtract_add_fusion.5, f32[]{:T(128)} %bitcast.17, f32[22,134]{1,0:T(8,128)S(1)} %copy-done.16, f32[16,22,134]{2,1,0:T(8,128)S(1)} %copy.651, f32[16,22,134]{2,1,0:T(8,128)S(1)} %copy.650, ...), kind=kLoop, calls=%fused_computation.708 | loop fusion | flops 5471488 | bytes 20062724 | tf_op jit(solution)/shard_map/sub | solution.py:134
  253.4 5.0 %multiply_subtract_fusion.4 = f32[2,16,20,132]{3,2,1,0:T(8,128)S(1)} fusion(f32[2,16,22,134]{3,2,1,0:T(8,128)S(1)} %multiply_subtract_fusion.5, f32[2,16,20,132]{3,2,1,0:T(8,128)S(1)} %subtract_add_fusion.4, f32[]{:T(128)} %bitcast.20, f32[20,132]{1,0:T(8,128)S(1)} %copy-done.15, f32[16,20,132]{2,1,0:T(8,128)S(1)} %copy.679, f32[16,20,132]{2,1,0:T(8,128)S(1)} %copy.678, ...), kind=kLoop, calls=%fused_computation.706 | loop fusion | flops 4899840 | bytes 20023300 | tf_op jit(solution)/shard_map/sub | solution.py:134
  267.0 4.8 %multiply_subtract_fusion.3 = f32[2,16,18,130]{3,2,1,0:T(8,128)S(1)} fusion(f32[2,16,20,132]{3,2,1,0:T(8,128)S(1)} %multiply_subtract_fusion.4, f32[2,16,18,130]{3,2,1,0:T(8,128)S(1)} %subtract_add_fusion.3, f32[]{:T(128)} %bitcast.23, f32[18,130]{1,0:T(8,128)S(1)} %copy-done.14, f32[16,18,130]{2,1,0:T(8,128)S(1)} %copy.707, f32[16,18,130]{2,1,0:T(8,128)S(1)} %copy.706, ...), kind=kLoop, calls=%fused_computation.704 | loop fusion | flops 4343040 | bytes 19984900 | tf_op jit(solution)/shard_map/sub | solution.py:134
  276.4 8.0 %stack.71 = f32[9,2,16,16,128]{4,0,3,2,1:T(8,128)} concatenate(f32[1,2,16,16,128]{4,0,3,2,1:T(1,128)S(1)} %bitcast.330, f32[1,2,16,16,128]{4,0,3,2,1:T(1,128)S(1)} %bitcast.336, f32[1,2,16,16,128]{4,0,3,2,1:T(1,128)S(1)} %bitcast.338, f32[1,2,16,16,128]{4,0,3,2,1:T(1,128)S(1)} %bitcast.340, f32[1,2,16,16,128]{4,0,3,2,1:T(1,128)S(1)} %bitcast.342, ...), dimensions={0} | concatenate | bytes 4718592 | tf_op jit(solution)/shard_map/stack | solution.py:144
  284.4 9.0 %convolution_bitcast_fusion = f32[9,9]{0,1:T(8,128)S(1)} fusion(f32[9,2,16,16,128]{4,0,3,2,1:T(8,128)} %stack.71), kind=kOutput, calls=%fused_computation.146 | convolution fusion | flops 63700992 | bytes 2359620 | tf_op jit(solution)/shard_map/dot_general | solution.py:140
  293.4 20.1 %psum.28 = f32[9,9]{0,1:T(8,128)S(1)} all-reduce(f32[9,9]{0,1:T(8,128)S(1)} %convolution_bitcast_fusion), channel_id=1, replica_groups=mesh['gx'=4,'gy'=8] {'gy'}, use_global_device_ids=true, to_apply=%region_0.1 | all-reduce | flops 81 | bytes 648 | tf_op jit(solution)/shard_map/psum | solution.py:141
  313.5 5.8 %psum.29 = f32[9,9]{0,1:T(8,128)S(1)} all-reduce(f32[9,9]{0,1:T(8,128)S(1)} %psum.28), channel_id=1, replica_groups=mesh['gx'=4,'gy'=8] {'gx'}, use_global_device_ids=true, to_apply=%region_1.2 | all-reduce | flops 81 | bytes 648 | tf_op jit(solution)/shard_map/psum | solution.py:141
  335.1 8.0 %stack.81 = f32[9,65536]{1,0:T(8,128)} concatenate(f32[1,65536]{1,0:T(1,128)S(1)} %bitcast.331, f32[1,65536]{1,0:T(1,128)S(1)} %bitcast.337, f32[1,65536]{1,0:T(1,128)S(1)} %bitcast.339, f32[1,65536]{1,0:T(1,128)S(1)} %bitcast.341, f32[1,65536]{1,0:T(1,128)S(1)} %bitcast.343, f32[1,65536]{1,0:T(1,128)S(1)} %bitcast.345, f32[1,65536]{1,0:T(1,128)S(1)} %bitcast.347, ...), dimensions={0} | concatenate | bytes 4718592 | tf_op jit(solution)/shard_map/stack | solution.py:144
  343.2 5.4 %fusion.1195 = f32[9,65536]{1,0:T(8,128)S(1)} fusion(f32[9,9]{1,0:T(8,128)S(1)} %scatter.74, f32[9,65536]{1,0:T(8,128)} %stack.81), kind=kOutput, calls=%fused_computation.1486 | convolution fusion | flops 63700992 | bytes 4718916 | tf_op jit(solution)/shard_map/dot_general | solution.py:96
  350.5 5.6 %fusion.1196 = f32[9,9]{0,1:T(8,128)S(1)} fusion(f32[9,65536]{1,0:T(8,128)S(1)} %fusion.1195), kind=kOutput, calls=%fused_computation.1487 | convolution fusion | flops 63700992 | bytes 2359620 | tf_op jit(solution)/shard_map/dot_general | solution.py:140
  356.1 17.4 %psum.30 = f32[9,9]{0,1:T(8,128)S(1)} all-reduce(f32[9,9]{0,1:T(8,128)S(1)} %fusion.1196), channel_id=1, replica_groups=mesh['gx'=4,'gy'=8] {'gy'}, use_global_device_ids=true, to_apply=%region_4.6 | all-reduce | flops 81 | bytes 648 | tf_op jit(solution)/shard_map/psum | solution.py:141
  373.5 5.9 %psum.31 = f32[9,9]{0,1:T(8,128)S(1)} all-reduce(f32[9,9]{0,1:T(8,128)S(1)} %psum.30), channel_id=1, replica_groups=mesh['gx'=4,'gy'=8] {'gx'}, use_global_device_ids=true, to_apply=%region_5.7 | all-reduce | flops 81 | bytes 648 | tf_op jit(solution)/shard_map/psum | solution.py:141
  396.1 5.4 %fusion.1197 = f32[9,65536]{1,0:T(8,128)S(1)} fusion(f32[9,9]{1,0:T(8,128)S(1)} %scatter.89, f32[9,65536]{1,0:T(8,128)} %copy-done), kind=kOutput, calls=%fused_computation.1488 | convolution fusion | flops 63700992 | bytes 4718916 | tf_op jit(solution)/shard_map/dot_general | solution.py:96
  (417 shorter events, 226.4 us)
Async XLA Ops:
  1.6 25.0 %collective-permute-start = (f32[2,16,8,128]{3,2,1,0:T(8,128)S(1)}, f32[2,16,8,128]{3,2,1,0:T(8,128)S(1)}, u32[]{:S(2)}, u32[]{:S(2)}) collective-permute-start(f32[2,16,8,128]{3,2,1,0:T(8,128)S(1)} %get-tuple-element.464), channel_id=1, source_target_pairs={{0,8},{8,16},{16,24},{1,9},{9,17},{17,25},{2,10},{10,18},{18,26},{... | collective-permute-start | bytes 393224 | tf_op jit(solution)/shard_map/ppermute | solution.py:16
  4.0 22.7 %collective-permute-start.1 = (f32[2,16,8,128]{3,2,1,0:T(8,128)S(1)}, f32[2,16,8,128]{3,2,1,0:T(8,128)S(1)}, u32[]{:S(2)}, u32[]{:S(2)}) collective-permute-start(f32[2,16,8,128]{3,2,1,0:T(8,128)S(1)} %get-tuple-element.463), channel_id=1, source_target_pairs={{8,0},{16,8},{24,16},{9,1},{17,9},{25,17},{10,2},{18,10},{26,18},{... | collective-permute-start | bytes 393224 | tf_op jit(solution)/shard_map/ppermute | solution.py:17
  6.4 19.5 %copy-start.23 = (f32[8]{0:T(128)S(1)}, f32[8]{0:T(128)}, u32[]{:S(2)}) copy-start(f32[8]{0:T(128)} %param.44) | copy-start | bytes 100
  6.4 20.2 %copy-start.1 = (f32[2,16,16,128]{3,2,1,0:T(8,128)S(1)}, f32[2,16,16,128]{3,2,1,0:T(8,128)}, u32[]{:S(2)}) copy-start(f32[2,16,16,128]{3,2,1,0:T(8,128)} %param.41) | copy-start | bytes 786436
  6.5 28.0 %collective-permute-start.5 = (f32[2,16,9,128]{3,1,2,0:T(8,128)S(1)}, f32[2,16,9,128]{3,1,2,0:T(8,128)S(1)}, u32[]{:S(2)}, u32[]{:S(2)}) collective-permute-start(f32[2,16,9,128]{3,1,2,0:T(8,128)S(1)} %copy.751), channel_id=1, source_target_pairs={{8,0},{16,8},{24,16},{9,1},{17,9},{25,17},{10,2},{18,10},{26,18},{... | collective-permute-start | bytes 442376 | tf_op jit(solution)/shard_map/ppermute | solution.py:17
  8.0 28.6 %collective-permute-start.4 = (f32[2,16,9,128]{3,1,2,0:T(8,128)S(1)}, f32[2,16,9,128]{3,1,2,0:T(8,128)S(1)}, u32[]{:S(2)}, u32[]{:S(2)}) collective-permute-start(f32[2,16,9,128]{3,1,2,0:T(8,128)S(1)} %copy.750), channel_id=1, source_target_pairs={{0,8},{8,16},{16,24},{1,9},{9,17},{17,25},{2,10},{10,18},{18,26},{... | collective-permute-start | bytes 442376 | tf_op jit(solution)/shard_map/ppermute | solution.py:16
  27.9 22.5 %collective-permute-start.3 = (f32[2,16,32,8]{3,2,1,0:T(8,128)}, f32[2,16,32,8]{3,2,1,0:T(8,128)}, u32[]{:S(2)}, u32[]{:S(2)}) collective-permute-start(f32[2,16,32,8]{3,2,1,0:T(8,128)} %get-tuple-element.460), channel_id=1, source_target_pairs={{1,0},{2,1},{3,2},{4,3},{5,4},{6,5},{7,6},{9,8},{10,9},{11,10},{12... | collective-permute-start | bytes 98312 | tf_op jit(solution)/shard_map/ppermute | solution.py:17
  29.1 30.0 %collective-permute-start.2 = (f32[2,16,32,8]{3,2,1,0:T(8,128)}, f32[2,16,32,8]{3,2,1,0:T(8,128)}, u32[]{:S(2)}, u32[]{:S(2)}) collective-permute-start(f32[2,16,32,8]{3,2,1,0:T(8,128)} %get-tuple-element.459), channel_id=1, source_target_pairs={{0,1},{1,2},{2,3},{3,4},{4,5},{5,6},{6,7},{8,9},{9,10},{10,11},{11... | collective-permute-start | bytes 98312 | tf_op jit(solution)/shard_map/ppermute | solution.py:16
  44.5 17.9 %collective-permute-start.7 = (f32[2,16,34,9]{2,1,3,0:T(8,128)}, f32[2,16,34,9]{2,1,3,0:T(8,128)S(1)}, u32[]{:S(2)}, u32[]{:S(2)}) collective-permute-start(f32[2,16,34,9]{2,1,3,0:T(8,128)} %get-tuple-element.440), channel_id=1, source_target_pairs={{1,0},{2,1},{3,2},{4,3},{5,4},{6,5},{7,6},{9,8},{10,9},{11,10},{12... | collective-permute-start | bytes 117512 | tf_op jit(solution)/shard_map/ppermute | solution.py:17
  45.8 17.0 %collective-permute-start.6 = (f32[2,16,34,9]{2,1,3,0:T(8,128)}, f32[2,16,34,9]{2,1,3,0:T(8,128)S(1)}, u32[]{:S(2)}, u32[]{:S(2)}) collective-permute-start(f32[2,16,34,9]{2,1,3,0:T(8,128)} %get-tuple-element.439), channel_id=1, source_target_pairs={{0,1},{1,2},{2,3},{3,4},{4,5},{5,6},{6,7},{8,9},{9,10},{10,11},{11... | collective-permute-start | bytes 117512 | tf_op jit(solution)/shard_map/ppermute | solution.py:16
  111.5 2.5 copy-start.4
  157.5 2.5 copy-start.5
  219.3 4.4 %copy-start.7 = (f32[16,24,136]{2,1,0:T(8,128)S(1)}, f32[16,24,136]{2,1,0:T(8,128)}, u32[]{:S(2)}) copy-start(f32[16,24,136]{2,1,0:T(8,128)} %copy.612) | copy-start | bytes 626692
  219.3 4.5 %copy-start.8 = (f32[16,24,136]{2,1,0:T(8,128)S(1)}, f32[16,24,136]{2,1,0:T(8,128)}, u32[]{:S(2)}) copy-start(f32[16,24,136]{2,1,0:T(8,128)} %copy.611) | copy-start | bytes 626692
  219.3 4.5 %copy-start.9 = (f32[16,24,136]{2,1,0:T(8,128)S(1)}, f32[16,24,136]{2,1,0:T(8,128)}, u32[]{:S(2)}) copy-start(f32[16,24,136]{2,1,0:T(8,128)} %copy.610) | copy-start | bytes 626692
  219.3 4.5 %copy-start.17 = (f32[24,136]{1,0:T(8,128)S(1)}, f32[24,136]{1,0:T(8,128)}, u32[]{:S(2)}) copy-start(f32[24,136]{1,0:T(8,128)} %slice.2776) | copy-start | bytes 39172
  220.3 3.5 copy-start.10
  221.3 2.5 copy-start.11
  267.0 5.1 %copy-start.28 = (pred[16,128]{1,0:T(8,128)(4,1)S(1)}, pred[16,128]{1,0:T(8,128)(4,1)}, u32[]{:S(2)}) copy-start(pred[16,128]{1,0:T(8,128)(4,1)} %broadcast_compare_fusion.7) | copy-start | bytes 6148
  274.4 2.0 copy-start.2
  321.6 3.2 copy-start.18
  348.5 2.0 copy-start
  350.5 31.9 %copy-start.19 = (f32[9,9]{1,0:T(8,128)S(1)}, f32[9,9]{1,0:T(8,128)}, u32[]{:S(2)}) copy-start(f32[9,9]{1,0:T(8,128)} %copy-done.18) | copy-start | bytes 976
  381.7 4.1 %copy-start.20 = (f32[9,9]{1,0:T(8,128)}, f32[9,9]{1,0:T(8,128)S(1)}, u32[]{:S(2)}) copy-start(f32[9,9]{1,0:T(8,128)S(1)} %select_select_fusion) | copy-start | bytes 976
  (13 other events, 15.6 us)
